TPU v7x, 32 devices: a whole 2x2x4 slice. The times are simulated.
32 devices in a mesh: row: 4 (over y, x), col: 4 (over z), rep: 2 (over core).
Axes of the slice: x: 2, y: 2, z: 4, core: 2. Of those that a mesh axis runs over, the one named last changes fastest.
Arguments:
- features: bfloat16 [2, 2048, 512], P('rep', ('row', 'col')), may hold values from -6 to 6
- cotangent: bfloat16 [2, 2048, 512], P('rep', ('row', 'col')), may hold values from -6 to 6
- weight: bfloat16 [512, 512], replicated, may hold values from -0.25 to 0.25
- tile_values: bfloat16 [2, 256, 128, 128], P('rep', ('row', 'col')), may hold values from -0.25 to 0.25
- tile_out: int32 [2, 256], P('rep', ('row', 'col')), may hold values from 0 to 3
- tile_in: int32 [2, 256], P('rep', ('row', 'col')), may hold values from 0 to 3
- tile_count: int32 [2, 16], P('rep', ('row', 'col')), may hold values from 8 to 16, as said below
Outputs:
- out_feats: bfloat16 [2, 2048, 512], P('rep', ('row', 'col'))
- grad_feats: bfloat16 [2, 2048, 512], P('rep', ('row', 'col'))
- grad_weight: float32 [512, 512], replicated
Inputs may be any that keep to these rules, and one draw needn't show every extreme that they name: `tile_count`: in each window some group has all 16 slots live.
All inputs are finite; a program needn't handle non-finite values.
Results may differ from a plain program's by a relative error of at most 0.015.
Values may be sent and summed in bfloat16 or wider, within the bound.
A program may use at most 64 MiB of HBM per device.

v0:
```python
import jax
import jax.numpy as jnp
from jax import lax
from jax.sharding import PartitionSpec as P

SECTIONS = 4


def passed_along(value, axis, steps):
    count = lax.axis_size(axis)
    leading, last = (max(0, -steps), min(count, count - steps))
    return lax.ppermute(value, axis, [(source, source + steps) for source in range(leading, last)])


def body(features, cotangent, weight, tile_values, tile_out, tile_in, tile_count):
    field_in = features[0]
    values = tile_values[0]
    outs_idx = tile_out[0]
    ins_idx = tile_in[0]
    count = tile_count[0, 0]
    node_rows, width = field_in.shape
    edge = values.shape[-1]
    per_span = node_rows // edge
    half = SECTIONS // 2
    col_count = lax.axis_size("col")
    out_count = col_count * per_span
    in_count = SECTIONS * per_span
    slot_total = values.shape[0]
    live = (jnp.arange(slot_total, dtype=jnp.int32) < count).astype(jnp.float32)
    out_hot = (outs_idx[None, :] == jnp.arange(out_count, dtype=jnp.int32)[:, None]).astype(
        jnp.float32
    ) * live[None, :]
    in_hot = (ins_idx[None, :] == jnp.arange(in_count, dtype=jnp.int32)[:, None]).astype(
        jnp.float32
    ) * live[None, :]
    pieces = []
    for section in range(SECTIONS):
        offset = section - half
        if offset == 0:
            pieces.append(field_in)
        else:
            pieces.append(passed_along(field_in, "row", -offset))
    blocks = jnp.stack(pieces)
    picked = blocks[ins_idx]
    prods = jnp.einsum("tij,tjf->tif", values, picked, preferred_element_type=jnp.float32)
    part = jnp.einsum("ot,tif->oif", out_hot, prods, precision=lax.Precision.HIGHEST)
    summed = lax.psum_scatter(
        part.reshape(out_count * edge, width).astype(jnp.bfloat16),
        "col",
        scatter_dimension=0,
        tiled=True,
    )
    pre = jnp.dot(summed, weight, preferred_element_type=jnp.float32)
    out_feats = jax.nn.silu(pre).astype(jnp.bfloat16)
    sigma = jax.nn.sigmoid(pre)
    dpre = (cotangent[0].astype(jnp.float32) * sigma * (1.0 + pre * (1.0 - sigma))).astype(
        jnp.bfloat16
    )
    local_grad = jnp.einsum("nf,ng->fg", summed, dpre, preferred_element_type=jnp.float32)
    total_nodes = node_rows * lax.axis_size("row") * col_count * lax.axis_size("rep")
    grad_weight = lax.psum(local_grad, ("row", "col", "rep")) * jnp.float32(total_nodes) ** (-0.5)
    dhidden = jnp.einsum("nf,gf->ng", dpre, weight, preferred_element_type=jnp.float32).astype(
        jnp.bfloat16
    )
    row_grads = lax.all_gather(dhidden, "col", axis=0, tiled=True).reshape(out_count, edge, width)
    chosen = row_grads[outs_idx]
    back_prods = jnp.einsum("tij,tif->tjf", values, chosen, preferred_element_type=jnp.float32)
    sections_part = jnp.einsum("it,tjf->ijf", in_hot, back_prods, precision=lax.Precision.HIGHEST)
    sections_part = sections_part.astype(jnp.bfloat16)
    total = jnp.zeros((node_rows, width), jnp.float32)
    for section in range(SECTIONS):
        offset = section - half
        if offset == 0:
            arrived = sections_part[section]
        else:
            arrived = passed_along(sections_part[section], "row", offset)
        total = total + arrived.astype(jnp.float32)
    grad_feats = total.astype(jnp.bfloat16)
    return (out_feats[None], grad_feats[None], grad_weight)


def solution(mesh):
    return jax.shard_map(
        body,
        mesh=mesh,
        in_specs=(
            P("rep", ("row", "col"), None),
            P("rep", ("row", "col"), None),
            P(),
            P("rep", ("row", "col"), None, None),
            P("rep", ("row", "col")),
            P("rep", ("row", "col")),
            P("rep", ("row", "col")),
        ),
        out_specs=(P("rep", ("row", "col"), None), P("rep", ("row", "col"), None), P()),
        check_vma=False,
    )
```

profile of v0, /device:TPU:0, one launch (start us, length us, event | category | flops | bytes accessed | tf_op | source)
XLA Modules:
  0.0 224.5 jit_solution(10835809086337116893)
XLA Ops:
  7.2 5.0 %collective-permute-start = (bf16[128,512]{1,0:T(8,128)(2,1)}, bf16[128,512]{1,0:T(8,128)(2,1)S(1)}, u32[]{:S(2)}, u32[]{:S(2)}) collective-permute-start(bf16[128,512]{1,0:T(8,128)(2,1)} %bitcast.76), channel_id=1, source_target_pairs={{0,16},{8,24},{1,17},{9,25},{2,18},{10,26},{3,19},{11,27},{4,20},{... | collective-permute-start | bytes 393224 | tf_op jit(solution)/shard_map/ppermute | solution.py:12
  12.2 3.4 %collective-permute-start.1 = (bf16[128,512]{1,0:T(8,128)(2,1)}, bf16[128,512]{1,0:T(8,128)(2,1)S(1)}, u32[]{:S(2)}, u32[]{:S(2)}) collective-permute-start(bf16[128,512]{1,0:T(8,128)(2,1)} %bitcast.77), channel_id=1, source_target_pairs={{0,8},{8,16},{16,24},{1,9},{9,17},{17,25},{2,10},{10,18},{18,26},{... | collective-permute-start | bytes 393224 | tf_op jit(solution)/shard_map/ppermute | solution.py:12
  15.7 1.3 collective-permute-start.2
  18.5 4.3 %collective-permute-done.2 = bf16[128,512]{1,0:T(8,128)(2,1)S(1)} collective-permute-done((bf16[128,512]{1,0:T(8,128)(2,1)}, bf16[128,512]{1,0:T(8,128)(2,1)S(1)}, u32[]{:S(2)}, u32[]{:S(2)}) %collective-permute-start.2) | collective-permute-done | bytes 131104 | tf_op jit(solution)/shard_map/ppermute | solution.py:12
  22.7 1.0 pad_maximum_fusion
  24.4 2.7 %fusion.12 = f32[16,512,128]{2,1,0:T(8,128)} fusion(bf16[16,128,512]{2,1,0:T(8,128)(2,1)S(1)} %gather_fusion, bf16[1,16,128,128]{3,2,1,0:T(8,128)(2,1)S(1)} %copy-done), kind=kOutput, calls=%fused_computation.12 | convolution fusion | flops 268435456 | bytes 6815744 | tf_op jit(solution)/shard_map/tij,tjf->tif/dot_general | solution.py:45
  27.1 5.5 %copy.16 = f32[16,512,128]{1,0,2:T(8,128)} copy(f32[16,512,128]{2,1,0:T(8,128)} %fusion.12) | data formatting | bytes 8388608 | tf_op jit(solution)/shard_map/tij,tjf->tif/dot_general | solution.py:45
  32.6 4.3 %fusion.4 = bf16[4,128,512]{2,0,1:T(4,128)(2,1)S(1)} fusion(f32[16,512,128]{1,0,2:T(8,128)} %copy.16, f32[16]{0:T(128)S(1)} %compare_convert_fusion, s32[16]{0:T(128)S(1)} %bitcast.82), kind=kOutput, calls=%fused_computation.6 | convolution fusion | flops 50593920 | bytes 4718720 | tf_op jit(solution)/shard_map/ot,tif->oif/dot_general | solution.py:46
  37.0 0.9 copy.13
  38.0 21.4 %reduce-scatter.2.cloned.1.call-done = bf16[128,512]{1,0:T(8,128)(2,1)} async-done(((bf16[512,512]{1,0:T(8,128)(2,1)}), bf16[128,512]{1,0:T(8,128)(2,1)}) %reduce-scatter.2.cloned.1.call-update) | async-done | bytes 131088 | tf_op jit(solution)/shard_map/reduce_scatter | solution.py:47
  59.4 1.1 fusion.38
  60.9 15.9 %all_gather.3 = bf16[512,512]{1,0:T(8,128)(2,1)S(1)} all-gather(bf16[128,512]{1,0:T(8,128)(2,1)S(1)} %convolution_convert_fusion), channel_id=1, replica_groups=mesh['row'=4,'col'=4,'rep'=2] {'col'}, dimensions={0}, use_global_device_ids=true | all-gather | bytes 655360 | tf_op jit(solution)/shard_map/all_gather | solution.py:65
  77.4 2.8 %fusion.10 = f32[16,512,128]{2,1,0:T(8,128)} fusion(bf16[16,128,512]{2,1,0:T(8,128)(2,1)S(1)} %gather_fusion.1, bf16[1,16,128,128]{3,2,1,0:T(8,128)(2,1)S(1)} %copy-done), kind=kOutput, calls=%fused_computation.10 | convolution fusion | flops 268435456 | bytes 6815744 | tf_op jit(solution)/shard_map/tij,tif->tjf/dot_general | solution.py:67
  80.2 5.5 %copy.17 = f32[16,512,128]{1,0,2:T(8,128)} copy(f32[16,512,128]{2,1,0:T(8,128)} %fusion.10) | data formatting | bytes 8388608 | tf_op jit(solution)/shard_map/tij,tif->tjf/dot_general | solution.py:67
  85.7 1.4 fusion.34
  87.1 4.3 %fusion.7 = bf16[4,128,512]{2,0,1:T(4,128)(2,1)S(1)} fusion(f32[16,512,128]{1,0,2:T(8,128)} %copy.17, s32[16]{0:T(128)S(1)} %bitcast.83, f32[16]{0:T(128)S(1)} %compare_convert_fusion), kind=kOutput, calls=%fused_computation.7 | convolution fusion | flops 50593920 | bytes 4718720 | tf_op jit(solution)/shard_map/it,tjf->ijf/dot_general | solution.py:68
  91.4 0.7 fusion.37
  92.1 1.3 collective-permute-start.3
  93.5 1.3 collective-permute-start.4
  94.8 4.6 %collective-permute-start.5 = (bf16[128,512]{1,0:T(8,128)(2,1)S(1)}, bf16[128,512]{1,0:T(8,128)(2,1)S(1)}, u32[]{:S(2)}, u32[]{:S(2)}) collective-permute-start(bf16[128,512]{1,0:T(8,128)(2,1)S(1)} %bitcast.75), channel_id=1, source_target_pairs={{0,8},{8,16},{16,24},{1,9},{9,17},{17,25},{2,10},{10,18},{18,26},{... | collective-permute-start | bytes 393224 | tf_op jit(solution)/shard_map/ppermute | solution.py:12
  99.4 0.7 fusion.19
  100.3 1.7 collective-permute-done.5
  102.7 112.6 %all-reduce.2.cloned.1.call-done = f32[512,512]{1,0:T(8,128)} async-done(((f32[512,512]{1,0:T(8,128)}), f32[512,512]{1,0:T(8,128)}) %all-reduce.2.cloned.1.call-update) | async-done | bytes 1048592 | tf_op jit(solution)/shard_map/psum | solution.py:61
  215.3 2.3 %broadcast_multiply_fusion = f32[512,512]{1,0:T(8,128)} fusion(f32[512,512]{1,0:T(8,128)} %all-reduce.2.cloned.1.call-done), kind=kLoop, calls=%fused_computation.14 | loop fusion | flops 262144 | bytes 2097152 | tf_op jit(solution)/shard_map/mul | solution.py:61
  (32 shorter events, 3.7 us)
Async XLA Ops:
  7.2 17.2 %copy-start = (bf16[1,16,128,128]{3,2,1,0:T(8,128)(2,1)S(1)}, bf16[1,16,128,128]{3,2,1,0:T(8,128)(2,1)}, u32[]{:S(2)}) copy-start(bf16[1,16,128,128]{3,2,1,0:T(8,128)(2,1)} %param.10) | copy-start | bytes 1572868
  7.2 52.2 %reduce-scatter.2.cloned.1.call-start = ((), (), s32[]{:S(2)}) async-start(), calls=%async_computation.1 | async-start | bytes 655360 | tf_op jit(solution)/shard_map/reduce_scatter | solution.py:47
  7.2 11.1 %collective-permute-start = (bf16[128,512]{1,0:T(8,128)(2,1)}, bf16[128,512]{1,0:T(8,128)(2,1)S(1)}, u32[]{:S(2)}, u32[]{:S(2)}) collective-permute-start(bf16[128,512]{1,0:T(8,128)(2,1)} %bitcast.76), channel_id=1, source_target_pairs={{0,16},{8,24},{1,17},{9,25},{2,18},{10,26},{3,19},{11,27},{4,20},{... | collective-permute-start | bytes 393224 | tf_op jit(solution)/shard_map/ppermute | solution.py:12
  12.2 6.2 %collective-permute-start.1 = (bf16[128,512]{1,0:T(8,128)(2,1)}, bf16[128,512]{1,0:T(8,128)(2,1)S(1)}, u32[]{:S(2)}, u32[]{:S(2)}) collective-permute-start(bf16[128,512]{1,0:T(8,128)(2,1)} %bitcast.77), channel_id=1, source_target_pairs={{0,8},{8,16},{16,24},{1,9},{9,17},{17,25},{2,10},{10,18},{18,26},{... | collective-permute-start | bytes 393224 | tf_op jit(solution)/shard_map/ppermute | solution.py:12
  15.7 7.1 %collective-permute-start.2 = (bf16[128,512]{1,0:T(8,128)(2,1)}, bf16[128,512]{1,0:T(8,128)(2,1)S(1)}, u32[]{:S(2)}, u32[]{:S(2)}) collective-permute-start(bf16[128,512]{1,0:T(8,128)(2,1)} %bitcast.78), channel_id=1, source_target_pairs={{8,0},{16,8},{24,16},{9,1},{17,9},{25,17},{10,2},{18,10},{26,18},{... | collective-permute-start | bytes 393224 | tf_op jit(solution)/shard_map/ppermute | solution.py:12
  27.1 5.5 %copy-start.3 = (s32[1,16]{1,0:T(1,128)S(1)}, s32[1,16]{1,0:T(1,128)}, u32[]{:S(2)}) copy-start(s32[1,16]{1,0:T(1,128)} %param.11) | copy-start | bytes 196
  32.6 26.8 %copy-start.1 = (bf16[512,512]{1,0:T(8,128)(2,1)S(1)}, bf16[512,512]{1,0:T(8,128)(2,1)}, u32[]{:S(2)}) copy-start(bf16[512,512]{1,0:T(8,128)(2,1)} %param.9) | copy-start | bytes 1572868
  37.0 23.6 %copy-start.5 = (bf16[1,128,512]{2,1,0:T(8,128)(2,1)S(1)}, bf16[1,128,512]{2,1,0:T(8,128)(2,1)}, u32[]{:S(2)}) copy-start(bf16[1,128,512]{2,1,0:T(8,128)(2,1)} %param.8) | copy-start | bytes 393220
  37.9 177.4 %all-reduce.2.cloned.1.call-start = ((), (), s32[]{:S(2)}) async-start(), calls=%async_computation.2 | async-start | bytes 2097152 | tf_op jit(solution)/shard_map/psum | solution.py:61
  80.2 5.5 %copy-start.2 = (bf16[128,512]{1,0:T(8,128)(2,1)S(1)}, bf16[128,512]{1,0:T(8,128)(2,1)}, u32[]{:S(2)}) copy-start(bf16[128,512]{1,0:T(8,128)(2,1)} %reduce-scatter.2.cloned.1.call-done) | copy-start | bytes 393220
  85.7 1.4 copy-start.4
  92.1 8.0 %collective-permute-start.3 = (bf16[128,512]{1,0:T(8,128)(2,1)S(1)}, bf16[128,512]{1,0:T(8,128)(2,1)S(1)}, u32[]{:S(2)}, u32[]{:S(2)}) collective-permute-start(bf16[128,512]{1,0:T(8,128)(2,1)S(1)} %bitcast.73), channel_id=1, source_target_pairs={{16,0},{24,8},{17,1},{25,9},{18,2},{26,10},{19,3},{27,11},{20,4},{... | collective-permute-start | bytes 393224 | tf_op jit(solution)/shard_map/ppermute | solution.py:12
  93.5 6.9 %collective-permute-start.4 = (bf16[128,512]{1,0:T(8,128)(2,1)S(1)}, bf16[128,512]{1,0:T(8,128)(2,1)S(1)}, u32[]{:S(2)}, u32[]{:S(2)}) collective-permute-start(bf16[128,512]{1,0:T(8,128)(2,1)S(1)} %bitcast.74), channel_id=1, source_target_pairs={{8,0},{16,8},{24,16},{9,1},{17,9},{25,17},{10,2},{18,10},{26,18},{... | collective-permute-start | bytes 393224 | tf_op jit(solution)/shard_map/ppermute | solution.py:12
  94.8 7.2 %collective-permute-start.5 = (bf16[128,512]{1,0:T(8,128)(2,1)S(1)}, bf16[128,512]{1,0:T(8,128)(2,1)S(1)}, u32[]{:S(2)}, u32[]{:S(2)}) collective-permute-start(bf16[128,512]{1,0:T(8,128)(2,1)S(1)} %bitcast.75), channel_id=1, source_target_pairs={{0,8},{8,16},{16,24},{1,9},{9,17},{17,25},{2,10},{10,18},{18,26},{... | collective-permute-start | bytes 393224 | tf_op jit(solution)/shard_map/ppermute | solution.py:12
Sparse Core Ops, SparseCore 0:
  38.0 21.3 reduce-scatter.1
  87.2 128.0 all-reduce.1
where the time goes:
time: 225 us; the launch traced here: 224 us
  waiting for transfers between devices  140 us (62%)
  starting transfers between devices  16.9 us (8%)
  matrix products  16.9 us (8%)
  blocking collectives  15.9 us (7%)
  between operations  14.9 us (7%)
  local copies, waits for them, and re-layouts  13.4 us (6%)
  other arithmetic  6.11 us (3%)
    psum x1, waiting for transfers between devices, body(): lax.psum(local_grad, ('row', 'col', 'rep'))  113 us
    reduce_scatter x1, waiting for transfers between devices, body(): lax.psum_scatter(part.reshape(out_count * edge, width).astype(jnp.bfloat1...  21.4 us
    ppermute x6, starting transfers between devices, passed_along(): lax.ppermute(value, axis, [(source, source + steps) for source in range(l...  16.8 us
    all_gather x1, blocking collectives, body(): lax.all_gather(dhidden, 'col', axis=0, tiled=True)  15.9 us
    ppermute x6, waiting for transfers between devices, passed_along(): lax.ppermute(value, axis, [(source, source + steps) for source in range(l...  6.33 us
    dot_general x1, local copies, waits for them, and re-layouts, body(): jnp.einsum('tij,tif->tjf', values, chosen, preferred_element_type=jnp.flo...  5.54 us
    dot_general x1, local copies, waits for them, and re-layouts, body(): jnp.einsum('tij,tjf->tif', values, picked, preferred_element_type=jnp.flo...  5.51 us
  transfers between devices with their start and end apart: 8, of which 6 were waited for; matrix products, arithmetic and copies ran while one was open for 3% of the time, Pallas kernels for 0%

commit v1 on v0

--- a/solution.py
+++ b/solution.py
@@ -2,6 +2,7 @@
 import jax.numpy as jnp
 from jax import lax
 from jax.sharding import PartitionSpec as P
+from jax.lax import psum
 
 SECTIONS = 4
 
@@ -58,7 +59,7 @@
     )
     local_grad = jnp.einsum("nf,ng->fg", summed, dpre, preferred_element_type=jnp.float32)
     total_nodes = node_rows * lax.axis_size("row") * col_count * lax.axis_size("rep")
-    grad_weight = lax.psum(local_grad, ("row", "col", "rep")) * jnp.float32(total_nodes) ** (-0.5)
+    grad_weight = psum(psum(local_grad, ("col", "rep")), "row") * jnp.float32(total_nodes) ** (-0.5)
     dhidden = jnp.einsum("nf,gf->ng", dpre, weight, preferred_element_type=jnp.float32).astype(
         jnp.bfloat16
     )

time: 225 us -> 190 us (0.84)
  waiting for transfers between devices: 140 us -> 104 us
    psum x1 -> x2, waiting for transfers between devices: 113 us -> 74 us  [the longest x1 41.3 us: body(): psum(psum(local_grad, ('col', 'rep')), 'row')]
    ppermute x6, waiting for transfers between devices: 6.33 us -> 8.58 us  [passed_along(): lax.ppermute(value, axis, [(source, source + steps) for source in range(l...]
  transfers between devices with their start and end apart: 8 -> 9, of which waited for: 6 -> 7; matrix products, arithmetic and copies ran while one was open for 3% -> 9% of each run, Pallas kernels for 0% -> 0%
where the time goes in v1:
time: 190 us; the launch traced here: 189 us
  waiting for transfers between devices  104 us (55%)
  blocking collectives  17.2 us (9%)
  starting transfers between devices  17 us (9%)
  matrix products  16.9 us (9%)
  between operations  14.6 us (8%)
  local copies, waits for them, and re-layouts  13.4 us (7%)
  other arithmetic  6.12 us (3%)
    psum x1, waiting for transfers between devices, body(): psum(psum(local_grad, ('col', 'rep')), 'row')  41.3 us
    psum x1, waiting for transfers between devices, body(): psum(local_grad, ('col', 'rep'))  32.7 us
    reduce_scatter x1, waiting for transfers between devices, body(): lax.psum_scatter(part.reshape(out_count * edge, width).astype(jnp.bfloat1...  21.4 us
    all_gather x1, blocking collectives, body(): lax.all_gather(dhidden, 'col', axis=0, tiled=True)  17.2 us
    ppermute x6, starting transfers between devices, passed_along(): lax.ppermute(value, axis, [(source, source + steps) for source in range(l...  16.8 us
    ppermute x6, waiting for transfers between devices, passed_along(): lax.ppermute(value, axis, [(source, source + steps) for source in range(l...  8.58 us
    dot_general x1, local copies, waits for them, and re-layouts, body(): jnp.einsum('tij,tif->tjf', values, chosen, preferred_element_type=jnp.flo...  5.52 us
    dot_general x1, local copies, waits for them, and re-layouts, body(): jnp.einsum('tij,tjf->tif', values, picked, preferred_element_type=jnp.flo...  5.51 us
  transfers between devices with their start and end apart: 9, of which 7 were waited for; matrix products, arithmetic and copies ran while one was open for 9% of the time, Pallas kernels for 0%

profile of v1, /device:TPU:0, one launch (start us, length us, event | category | flops | bytes accessed | tf_op | source)
XLA Modules:
  0.0 189.2 jit_solution(15324118576987524190)
XLA Ops:
  7.2 5.0 %collective-permute-start = (bf16[128,512]{1,0:T(8,128)(2,1)}, bf16[128,512]{1,0:T(8,128)(2,1)S(1)}, u32[]{:S(2)}, u32[]{:S(2)}) collective-permute-start(bf16[128,512]{1,0:T(8,128)(2,1)} %bitcast.76), channel_id=1, source_target_pairs={{0,16},{8,24},{1,17},{9,25},{2,18},{10,26},{3,19},{11,27},{4,20},{... | collective-permute-start | bytes 393224 | tf_op jit(solution)/shard_map/ppermute | solution.py:13
  12.2 3.4 %collective-permute-start.1 = (bf16[128,512]{1,0:T(8,128)(2,1)}, bf16[128,512]{1,0:T(8,128)(2,1)S(1)}, u32[]{:S(2)}, u32[]{:S(2)}) collective-permute-start(bf16[128,512]{1,0:T(8,128)(2,1)} %bitcast.77), channel_id=1, source_target_pairs={{0,8},{8,16},{16,24},{1,9},{9,17},{17,25},{2,10},{10,18},{18,26},{... | collective-permute-start | bytes 393224 | tf_op jit(solution)/shard_map/ppermute | solution.py:13
  15.7 1.3 collective-permute-start.2
  18.5 4.3 %collective-permute-done.2 = bf16[128,512]{1,0:T(8,128)(2,1)S(1)} collective-permute-done((bf16[128,512]{1,0:T(8,128)(2,1)}, bf16[128,512]{1,0:T(8,128)(2,1)S(1)}, u32[]{:S(2)}, u32[]{:S(2)}) %collective-permute-start.2) | collective-permute-done | bytes 131104 | tf_op jit(solution)/shard_map/ppermute | solution.py:13
  22.7 1.0 pad_maximum_fusion
  24.4 2.7 %fusion.12 = f32[16,512,128]{2,1,0:T(8,128)} fusion(bf16[16,128,512]{2,1,0:T(8,128)(2,1)S(1)} %gather_fusion, bf16[1,16,128,128]{3,2,1,0:T(8,128)(2,1)S(1)} %copy-done), kind=kOutput, calls=%fused_computation.12 | convolution fusion | flops 268435456 | bytes 6815744 | tf_op jit(solution)/shard_map/tij,tjf->tif/dot_general | solution.py:46
  27.1 5.5 %copy.16 = f32[16,512,128]{1,0,2:T(8,128)} copy(f32[16,512,128]{2,1,0:T(8,128)} %fusion.12) | data formatting | bytes 8388608 | tf_op jit(solution)/shard_map/tij,tjf->tif/dot_general | solution.py:46
  32.6 4.3 %fusion.4 = bf16[4,128,512]{2,0,1:T(4,128)(2,1)S(1)} fusion(f32[16,512,128]{1,0,2:T(8,128)} %copy.16, f32[16]{0:T(128)S(1)} %compare_convert_fusion, s32[16]{0:T(128)S(1)} %bitcast.82), kind=kOutput, calls=%fused_computation.6 | convolution fusion | flops 50593920 | bytes 4718720 | tf_op jit(solution)/shard_map/ot,tif->oif/dot_general | solution.py:47
  37.0 0.9 copy.13
  38.0 21.4 %reduce-scatter.2.cloned.1.call-done = bf16[128,512]{1,0:T(8,128)(2,1)} async-done(((bf16[512,512]{1,0:T(8,128)(2,1)}), bf16[128,512]{1,0:T(8,128)(2,1)}) %reduce-scatter.2.cloned.1.call-update) | async-done | bytes 131088 | tf_op jit(solution)/shard_map/reduce_scatter | solution.py:48
  59.4 1.2 fusion.38
  61.0 1.3 fusion.34
  62.4 17.2 %all_gather.3 = bf16[512,512]{1,0:T(8,128)(2,1)S(1)} all-gather(bf16[128,512]{1,0:T(8,128)(2,1)S(1)} %convolution_convert_fusion), channel_id=1, replica_groups=mesh['row'=4,'col'=4,'rep'=2] {'col'}, dimensions={0}, use_global_device_ids=true | all-gather | bytes 655360 | tf_op jit(solution)/shard_map/all_gather | solution.py:66
  80.3 2.8 %fusion.10 = f32[16,512,128]{2,1,0:T(8,128)} fusion(bf16[16,128,512]{2,1,0:T(8,128)(2,1)S(1)} %gather_fusion.1, bf16[1,16,128,128]{3,2,1,0:T(8,128)(2,1)S(1)} %copy-done), kind=kOutput, calls=%fused_computation.10 | convolution fusion | flops 268435456 | bytes 6815744 | tf_op jit(solution)/shard_map/tij,tif->tjf/dot_general | solution.py:68
  83.0 5.5 %copy.17 = f32[16,512,128]{1,0,2:T(8,128)} copy(f32[16,512,128]{2,1,0:T(8,128)} %fusion.10) | data formatting | bytes 8388608 | tf_op jit(solution)/shard_map/tij,tif->tjf/dot_general | solution.py:68
  88.5 32.7 %all-reduce.3.cloned.1.call-done = f32[512,512]{1,0:T(8,128)} async-done(((f32[512,512]{1,0:T(8,128)}), f32[512,512]{1,0:T(8,128)}) %all-reduce.3.cloned.1.call-update) | async-done | bytes 1048592 | tf_op jit(solution)/shard_map/psum | solution.py:62
  121.3 4.3 %fusion.7 = bf16[4,128,512]{2,0,1:T(4,128)(2,1)S(1)} fusion(f32[16,512,128]{1,0,2:T(8,128)} %copy.17, s32[16]{0:T(128)S(1)} %bitcast.83, f32[16]{0:T(128)S(1)} %compare_convert_fusion), kind=kOutput, calls=%fused_computation.7 | convolution fusion | flops 50593920 | bytes 4718720 | tf_op jit(solution)/shard_map/it,tjf->ijf/dot_general | solution.py:69
  126.3 1.3 collective-permute-start.3
  127.7 1.3 collective-permute-start.4
  129.0 4.6 %collective-permute-start.5 = (bf16[128,512]{1,0:T(8,128)(2,1)S(1)}, bf16[128,512]{1,0:T(8,128)(2,1)S(1)}, u32[]{:S(2)}, u32[]{:S(2)}) collective-permute-start(bf16[128,512]{1,0:T(8,128)(2,1)S(1)} %bitcast.75), channel_id=1, source_target_pairs={{0,8},{8,16},{16,24},{1,9},{9,17},{17,25},{2,10},{10,18},{18,26},{... | collective-permute-start | bytes 393224 | tf_op jit(solution)/shard_map/ppermute | solution.py:13
  134.3 1.4 collective-permute-done.3
  135.7 2.7 %collective-permute-done.4 = bf16[128,512]{1,0:T(8,128)(2,1)S(1)} collective-permute-done((bf16[128,512]{1,0:T(8,128)(2,1)S(1)}, bf16[128,512]{1,0:T(8,128)(2,1)S(1)}, u32[]{:S(2)}, u32[]{:S(2)}) %collective-permute-start.4) | collective-permute-done | bytes 131104 | tf_op jit(solution)/shard_map/ppermute | solution.py:13
  139.2 41.3 %all-reduce.5.cloned.1.call-done = f32[512,512]{1,0:T(8,128)} async-done(((f32[512,512]{1,0:T(8,128)}), f32[512,512]{1,0:T(8,128)}) %all-reduce.5.cloned.1.call-update) | async-done | bytes 1048592 | tf_op jit(solution)/shard_map/psum | solution.py:62
  180.4 2.3 %broadcast_multiply_fusion = f32[512,512]{1,0:T(8,128)} fusion(f32[512,512]{1,0:T(8,128)} %all-reduce.5.cloned.1.call-done), kind=kLoop, calls=%fused_computation.14 | loop fusion | flops 262144 | bytes 2097152 | tf_op jit(solution)/shard_map/mul | solution.py:62
  (35 shorter events, 5.0 us)
Async XLA Ops:
  7.2 17.2 %copy-start = (bf16[1,16,128,128]{3,2,1,0:T(8,128)(2,1)S(1)}, bf16[1,16,128,128]{3,2,1,0:T(8,128)(2,1)}, u32[]{:S(2)}) copy-start(bf16[1,16,128,128]{3,2,1,0:T(8,128)(2,1)} %param.10) | copy-start | bytes 1572868
  7.2 52.2 %reduce-scatter.2.cloned.1.call-start = ((), (), s32[]{:S(2)}) async-start(), calls=%async_computation.1 | async-start | bytes 655360 | tf_op jit(solution)/shard_map/reduce_scatter | solution.py:48
  7.2 11.1 %collective-permute-start = (bf16[128,512]{1,0:T(8,128)(2,1)}, bf16[128,512]{1,0:T(8,128)(2,1)S(1)}, u32[]{:S(2)}, u32[]{:S(2)}) collective-permute-start(bf16[128,512]{1,0:T(8,128)(2,1)} %bitcast.76), channel_id=1, source_target_pairs={{0,16},{8,24},{1,17},{9,25},{2,18},{10,26},{3,19},{11,27},{4,20},{... | collective-permute-start | bytes 393224 | tf_op jit(solution)/shard_map/ppermute | solution.py:13
  12.2 6.2 %collective-permute-start.1 = (bf16[128,512]{1,0:T(8,128)(2,1)}, bf16[128,512]{1,0:T(8,128)(2,1)S(1)}, u32[]{:S(2)}, u32[]{:S(2)}) collective-permute-start(bf16[128,512]{1,0:T(8,128)(2,1)} %bitcast.77), channel_id=1, source_target_pairs={{0,8},{8,16},{16,24},{1,9},{9,17},{17,25},{2,10},{10,18},{18,26},{... | collective-permute-start | bytes 393224 | tf_op jit(solution)/shard_map/ppermute | solution.py:13
  15.7 7.1 %collective-permute-start.2 = (bf16[128,512]{1,0:T(8,128)(2,1)}, bf16[128,512]{1,0:T(8,128)(2,1)S(1)}, u32[]{:S(2)}, u32[]{:S(2)}) collective-permute-start(bf16[128,512]{1,0:T(8,128)(2,1)} %bitcast.78), channel_id=1, source_target_pairs={{8,0},{16,8},{24,16},{9,1},{17,9},{25,17},{10,2},{18,10},{26,18},{... | collective-permute-start | bytes 393224 | tf_op jit(solution)/shard_map/ppermute | solution.py:13
  27.1 5.5 %copy-start.3 = (s32[1,16]{1,0:T(1,128)S(1)}, s32[1,16]{1,0:T(1,128)}, u32[]{:S(2)}) copy-start(s32[1,16]{1,0:T(1,128)} %param.11) | copy-start | bytes 196
  32.6 26.8 %copy-start.1 = (bf16[512,512]{1,0:T(8,128)(2,1)S(1)}, bf16[512,512]{1,0:T(8,128)(2,1)}, u32[]{:S(2)}) copy-start(bf16[512,512]{1,0:T(8,128)(2,1)} %param.9) | copy-start | bytes 1572868
  37.0 23.6 %copy-start.5 = (bf16[1,128,512]{2,1,0:T(8,128)(2,1)S(1)}, bf16[1,128,512]{2,1,0:T(8,128)(2,1)}, u32[]{:S(2)}) copy-start(bf16[1,128,512]{2,1,0:T(8,128)(2,1)} %param.8) | copy-start | bytes 393220
  37.9 83.3 %all-reduce.3.cloned.1.call-start = ((), (), s32[]{:S(2)}) async-start(), calls=%async_computation.2 | async-start | bytes 2097152 | tf_op jit(solution)/shard_map/psum | solution.py:62
  59.4 1.5 copy-start.2
  62.3 118.1 %all-reduce.5.cloned.1.call-start = ((), (), s32[]{:S(2)}) async-start(), calls=%async_computation.3 | async-start | bytes 2097152 | tf_op jit(solution)/shard_map/psum | solution.py:62
  83.0 38.3 %copy-start.4 = (s32[1,16]{1,0:T(1,128)S(1)}, s32[1,16]{1,0:T(1,128)}, u32[]{:S(2)}) copy-start(s32[1,16]{1,0:T(1,128)} %param.12) | copy-start | bytes 196
  126.3 9.4 %collective-permute-start.3 = (bf16[128,512]{1,0:T(8,128)(2,1)S(1)}, bf16[128,512]{1,0:T(8,128)(2,1)S(1)}, u32[]{:S(2)}, u32[]{:S(2)}) collective-permute-start(bf16[128,512]{1,0:T(8,128)(2,1)S(1)} %bitcast.73), channel_id=1, source_target_pairs={{16,0},{24,8},{17,1},{25,9},{18,2},{26,10},{19,3},{27,11},{20,4},{... | collective-permute-start | bytes 393224 | tf_op jit(solution)/shard_map/ppermute | solution.py:13
  127.7 10.8 %collective-permute-start.4 = (bf16[128,512]{1,0:T(8,128)(2,1)S(1)}, bf16[128,512]{1,0:T(8,128)(2,1)S(1)}, u32[]{:S(2)}, u32[]{:S(2)}) collective-permute-start(bf16[128,512]{1,0:T(8,128)(2,1)S(1)} %bitcast.74), channel_id=1, source_target_pairs={{8,0},{16,8},{24,16},{9,1},{17,9},{25,17},{10,2},{18,10},{26,18},{... | collective-permute-start | bytes 393224 | tf_op jit(solution)/shard_map/ppermute | solution.py:13
  129.0 9.5 %collective-permute-start.5 = (bf16[128,512]{1,0:T(8,128)(2,1)S(1)}, bf16[128,512]{1,0:T(8,128)(2,1)S(1)}, u32[]{:S(2)}, u32[]{:S(2)}) collective-permute-start(bf16[128,512]{1,0:T(8,128)(2,1)S(1)} %bitcast.75), channel_id=1, source_target_pairs={{0,8},{8,16},{16,24},{1,9},{9,17},{17,25},{2,10},{10,18},{18,26},{... | collective-permute-start | bytes 393224 | tf_op jit(solution)/shard_map/ppermute | solution.py:13
Sparse Core Ops, SparseCore 0:
  38.0 21.3 reduce-scatter.1
  62.4 58.7 all-reduce.2
  124.3 56.0 all-reduce.4
